TPU v7x, 32 devices: a whole 2x2x4 slice. The times are simulated.
32 devices in a mesh: row: 4 (over z), col: 4 (over y, x), pair: 2 (over core).
Axes of the slice: x: 2, y: 2, z: 4, core: 2. Of those that a mesh axis runs over, the one named last changes fastest.
Arguments:
- integrals: bfloat16 [2048, 2048], P('row', ('col', 'pair')), may hold values from -0.1875 to 0.1875
- int_mask: int32 [32, 32], P('row', ('col', 'pair')), may hold values 0 or 1
- amplitudes: bfloat16 [2048, 2048], P('row', ('col', 'pair')), may hold values from -6 to 6
- domain_mask: int32 [32, 2048], P('row', ('col', 'pair')), may hold values 0 or 1
- virt_energy: float32 [2048], P('row'), may hold values from 0.5 to 4
- occ_energy: float32 [2048], P(('col', 'pair')), may hold values from -3 to -0.5
Outputs:
- update: float32 [2048, 2048], P('row', ('col', 'pair'))
All inputs are finite; a program needn't handle non-finite values. No bound on the sum of `int_mask` or of `domain_mask` on one device may be relied on, other than what follows from the above.
Results may differ from a plain program's by a relative error of at most 0.0003.
Values may be sent and summed in bfloat16 or wider, within the bound.
A program may use at most 64 MiB of HBM per device.

v0:
```python
import jax
import jax.numpy as jnp
from jax import lax
from jax.sharding import PartitionSpec as P

TILE = 64


def mask_tiles(values, tile_mask):
    shaped = values.reshape(tile_mask.shape[0], TILE, tile_mask.shape[1], TILE)
    return (shaped * tile_mask[:, None, :, None].astype(values.dtype)).reshape(values.shape)


def mask_rows(values, row_mask):
    shaped = values.reshape(row_mask.shape[0], TILE, values.shape[1])
    return (shaped * row_mask[:, None, :].astype(values.dtype)).reshape(values.shape)


def local(integrals, int_mask, amplitudes, domain_mask, virt_energy, occ_energy):
    masked_ints = mask_tiles(integrals, int_mask)
    masked_amps = mask_rows(amplitudes, domain_mask)
    amps_whole = lax.all_gather(masked_amps, "row", axis=0, tiled=True)
    ladder = jnp.dot(
        lax.all_gather(masked_ints, ("col", "pair"), axis=1, tiled=True),
        amps_whole,
        preferred_element_type=jnp.float32,
    )
    denominator = virt_energy[:, None] - occ_energy[None, :]
    scaled = ladder / denominator
    return mask_rows(scaled, domain_mask)


def solution(mesh):
    placed = (
        P("row", ("col", "pair")),
        P("row", ("col", "pair")),
        P("row", ("col", "pair")),
        P("row", ("col", "pair")),
        P("row"),
        P(("col", "pair")),
    )
    return jax.shard_map(
        local, mesh=mesh, in_specs=placed, out_specs=P("row", ("col", "pair")), check_vma=False
    )
```

profile of v0, /device:TPU:0, one launch (start us, length us, event | category | flops | bytes accessed | tf_op | source)
XLA Modules:
  0.0 79.7 jit_solution(4837821829733445716)
XLA Ops:
  6.5 0.0 copy-start
  6.5 0.0 copy-start.2
  6.5 0.0 copy-start.1
  6.5 0.0 all-gather.5.cloned.1.call-start
  6.5 0.8 fusion.1
  7.3 1.7 %bitcast_multiply_fusion = bf16[512,256]{1,0:T(8,128)(2,1)} fusion(bf16[512,256]{1,0:T(8,128)(2,1)} %param.8, bf16[8,256]{1,0:T(8,128)(2,1)S(1)} %get-tuple-element.5), kind=kLoop, calls=%fused_computation.2 | loop fusion | flops 131072 | bytes 528384 | tf_op jit(solution)/shard_map/mul | solution.py:16
  9.0 0.0 all-gather.5.cloned.1.call-update
  9.0 0.0 all-gather.3.cloned.1.call-start
  9.1 0.7 convert_element_type.12
  9.8 0.1 copy.7
  9.9 0.2 mul.33
  10.1 0.3 mul.34
  10.4 0.0 copy-done
  10.4 0.8 mul.35
  11.2 0.0 all-gather.3.cloned.1.call-update
  11.2 28.6 %all-gather.5.cloned.1.call-done = bf16[2048,256]{1,0:T(8,128)(2,1)} async-done(((bf16[512,256]{1,0:T(8,128)(2,1)}), bf16[2048,256]{1,0:T(8,128)(2,1)}) %all-gather.5.cloned.1.call-update) | async-done | bytes 1048592 | tf_op jit(solution)/shard_map/all_gather | solution.py:22
  39.8 29.6 %all-gather.3.cloned.1.call-done = bf16[512,2048]{1,0:T(8,128)(2,1)} async-done(((bf16[512,256]{1,0:T(8,128)(2,1)}), bf16[512,2048]{1,0:T(8,128)(2,1)}) %all-gather.3.cloned.1.call-update) | async-done | bytes 2097168 | tf_op jit(solution)/shard_map/all_gather | solution.py:24
  69.4 0.0 copy-done.2
  69.5 0.0 copy-done.1
  69.5 3.4 %fusion = f32[512,256]{1,0:T(8,128)} fusion(f32[512,256]{1,0:T(8,128)S(1)} %bitcast.5, bf16[512,2048]{1,0:T(8,128)(2,1)} %all-gather.3.cloned.1.call-done, bf16[2048,256]{1,0:T(8,128)(2,1)} %all-gather.5.cloned.1.call-done, f32[256]{0:T(256)S(1)} %copy-done.2, f32[512]{0:T(512)S(1)} %copy-done.1), kind=kOutput, calls=%fused_computation.1 | convolution fusion | flops 537264128 | bytes 4197376 | tf_op jit(solution)/shard_map/dot_general | solution.py:23
  (1 shorter events, 0.0 us)
Async XLA Ops:
  6.5 3.9 %copy-start = (bf16[512,256]{1,0:T(8,128)(2,1)S(1)}, bf16[512,256]{1,0:T(8,128)(2,1)}, u32[]{:S(2)}) copy-start(bf16[512,256]{1,0:T(8,128)(2,1)} %param.6) | copy-start | bytes 786436
  6.5 62.9 %copy-start.2 = (f32[256]{0:T(256)S(1)}, f32[256]{0:T(256)}, u32[]{:S(2)}) copy-start(f32[256]{0:T(256)} %param.11) | copy-start | bytes 3076
  6.5 62.9 %copy-start.1 = (f32[512]{0:T(512)S(1)}, f32[512]{0:T(512)}, u32[]{:S(2)}) copy-start(f32[512]{0:T(512)} %param.10) | copy-start | bytes 6148
  6.5 33.3 %all-gather.5.cloned.1.call-start = ((), (), s32[]{:S(2)}) async-start(), calls=%async_computation.1 | async-start | bytes 1310720 | tf_op jit(solution)/shard_map/all_gather | solution.py:22
  9.0 60.4 %all-gather.3.cloned.1.call-start = ((), (), s32[]{:S(2)}) async-start(), calls=%async_computation | async-start | bytes 2359296 | tf_op jit(solution)/shard_map/all_gather | solution.py:24
Sparse Core Ops, SparseCore 0:
  9.1 30.6 all-gather.4
  41.7 27.6 all-gather.2
where the time goes:
time: 79.9 us; the launch traced here: 79.7 us
  waiting for transfers between devices  58.2 us (73%)
  between operations  13.4 us (17%)
  other arithmetic  3.9 us (5%)
  matrix products  3.37 us (4%)
    all_gather x1, waiting for transfers between devices, local(): lax.all_gather(masked_ints, ('col', 'pair'), axis=1, tiled=True)  29.6 us
    all_gather x1, waiting for transfers between devices, local(): amps_whole = lax.all_gather(masked_amps, 'row', axis=0, tiled=True)  28.6 us
    dot_general x1, matrix products, local(): jnp.dot(lax.all_gather(masked_ints, ('col', 'pair'), axis=1, tiled=True),...  3.37 us
    mul x1, other arithmetic, mask_rows(): shaped * row_mask[:, None, :].astype(values.dtype)  1.67 us
  transfers between devices with their start and end apart: 2, of which 2 were waited for; matrix products, arithmetic and copies ran while one was open for 3% of the time, Pallas kernels for 0%

commit v1 on v0

v1 whole, which is shorter than its diff:
```python
import functools

import jax
import jax.numpy as jnp
from jax import lax
from jax.experimental import pallas as pl
from jax.experimental.pallas import tpu as pltpu
from jax.sharding import PartitionSpec as P

TILE = 64
MESH = pl.DeviceIdType.MESH


def flipped(index, distance, count):
    out, bit = 0, 1
    while bit < count:
        have = lax.rem(index // bit, 2)
        out = out + bit * (1 - have if (distance // bit) % 2 else have)
        bit *= 2
    return out


def kernel(R, C, a_hbm, im_ref, b_hbm, dm_ref, v_ref, o_ref, out_ref,
           a_all, b_all, acc, inv, load_sem, a_send, a_recv, sib_send, sib_recv,
           dn_send, dn_recv, up_send, up_recv):
    r, c, p = lax.axis_index("row"), lax.axis_index("col"), lax.axis_index("pair")
    q = 1 - p
    rows, width = a_hbm.shape
    depth, cols = b_hbm.shape
    parts = depth // width
    tiles = depth // TILE

    load_b = pltpu.make_async_copy(b_hbm, b_all.at[r], load_sem.at[0])
    load_a = pltpu.make_async_copy(a_hbm, a_all.at[c * 2 + p], load_sem.at[1])
    load_b.start()
    load_a.start()

    others = [flipped(c, d, C) for d in range(C)]
    barrier = pltpu.get_barrier_semaphore()

    def greet(device):
        pl.semaphore_signal(barrier, inc=1, device_id=device, device_id_type=MESH)

    greet((r, c, q))
    for d in range(1, C):
        greet((r, others[d], p))

    @pl.when(r > 0)
    def _():
        greet((r - 1, c, p))

    @pl.when(r < R - 1)
    def _():
        greet((r + 1, c, p))

    def part(block, j):
        return b_all.at[block, pl.ds(j * width, width)]

    def down(block, s, j):
        return pltpu.make_async_remote_copy(
            src_ref=part(block, j), dst_ref=part(block, j),
            send_sem=dn_send.at[s, j], recv_sem=dn_recv.at[s, j],
            device_id=(r - 1, c, p), device_id_type=MESH)

    def up(block, s, j):
        return pltpu.make_async_remote_copy(
            src_ref=part(block, j), dst_ref=part(block, j),
            send_sem=up_send.at[s, j], recv_sem=up_recv.at[s, j],
            device_id=(r + 1, c, p), device_id_type=MESH)

    def across(d):
        slot = a_all.at[c * 2 + p]
        return pltpu.make_async_remote_copy(
            src_ref=slot, dst_ref=slot, send_sem=a_send.at[d], recv_sem=a_recv.at[d],
            device_id=(r, others[d], p), device_id_type=MESH)

    def sibling(d):
        slot = a_all.at[others[d] * 2 + p]
        return pltpu.make_async_remote_copy(
            src_ref=slot, dst_ref=slot, send_sem=sib_send.at[d], recv_sem=sib_recv.at[d],
            device_id=(r, c, q), device_id_type=MESH)

    load_b.wait()
    for t in range(tiles):
        keep = dm_ref[t:t + 1, :].astype(jnp.bfloat16)
        here = pl.ds(t * TILE, TILE)
        b_all[r, here, :] = b_all[r, here, :] * keep

    pl.semaphore_wait(barrier, C + (r + R - 1) // R + (2 * R - 2 - r) // R)

    for j in range(parts):
        @pl.when(r > 0)
        def _():
            down(r, 0, j).start()

        @pl.when(r < R - 1)
        def _():
            up(r, 0, j).start()

    load_a.wait()
    lane = lax.broadcasted_iota(jnp.int32, (rows // TILE, width), 1) // TILE
    wide = jnp.zeros((rows // TILE, width), jnp.int32)
    for t in range(width // TILE):
        wide = jnp.where(lane == t, im_ref[:, t:t + 1], wide)
    wide = wide.astype(jnp.float32)
    me = c * 2 + p
    for t in range(rows // TILE):
        here = pl.ds(t * TILE, TILE)
        a_all[me, here, :] = a_all[me, here, :] * wide[t:t + 1, :].astype(jnp.bfloat16)

    for d in range(1, C):
        across(d).start()
    sibling(0).start()

    for t in range(rows // 128):
        v = jnp.broadcast_to(v_ref[:, t * 128:(t + 1) * 128], (128, 128)).T
        for u in range(cols // 128):
            lanes = slice(u * 128, (u + 1) * 128)
            factor = 1.0 / (v - o_ref[:, lanes])
            for w in range(128 // TILE):
                row = t * (128 // TILE) + w
                keep = dm_ref[row:row + 1, lanes].astype(jnp.float32)
                inv[pl.ds(row * TILE, TILE), lanes] = factor[w * TILE:(w + 1) * TILE] * keep

    def receive(s, j):
        above, below = r + s + 1, r - s - 1

        @pl.when(above < R)
        def _():
            down(above, s, j).wait_recv()

            @pl.when(r > 0)
            def _():
                down(above, s + 1, j).start()

        @pl.when(below >= 0)
        def _():
            up(below, s, j).wait_recv()

            @pl.when(r < R - 1)
            def _():
                up(below, s + 1, j).start()

    def product(block, j):
        return jnp.dot(a_all[block * parts + j], b_all[block, j * width:(j + 1) * width],
                       preferred_element_type=jnp.float32)

    def add(block, j):
        acc[...] += product(block, j)

    for j in range(parts):
        receive(0, j)
    for d in range(1, C):
        across(d).wait_recv()
        sibling(d).start()
    for d in range(C):
        pltpu.make_async_remote_copy(
            src_ref=a_all.at[others[d] * 2 + q], dst_ref=a_all.at[others[d] * 2 + q],
            send_sem=sib_send.at[d], recv_sem=sib_recv.at[d],
            device_id=(r, c, q), device_id_type=MESH).wait_recv()

    acc[...] = product(r, 0)
    for j in range(1, parts):
        add(r, j)

    for s in range(R - 1):
        for j in range(parts):
            if s > 0:
                receive(s, j)

            @pl.when(r + s + 1 < R)
            def _():
                add(r + s + 1, j)

            @pl.when(r - s - 1 >= 0)
            def _():
                add(r - s - 1, j)

    out_ref[...] = acc[...] * inv[...]

    for d in range(1, C):
        across(d).wait_send()
    for d in range(C):
        sibling(d).wait_send()
    for s in range(R - 1):
        for j in range(parts):
            @pl.when((r + s < R) & (r > 0))
            def _():
                down(r + s, s, j).wait_send()

            @pl.when((r - s >= 0) & (r < R - 1))
            def _():
                up(r - s, s, j).wait_send()


def solution(mesh):
    R, C = mesh.shape["row"], mesh.shape["col"]

    def local(integrals, int_mask, amplitudes, domain_mask, virt_energy, occ_energy):
        rows, width = integrals.shape
        depth, cols = amplitudes.shape
        parts = depth // width
        vmem = pl.BlockSpec(memory_space=pltpu.VMEM)
        hbm = pl.BlockSpec(memory_space=pl.ANY)
        dma = pltpu.SemaphoreType.DMA
        return pl.pallas_call(
            functools.partial(kernel, R, C),
            out_shape=jax.ShapeDtypeStruct((rows, cols), jnp.float32),
            in_specs=[hbm, vmem, hbm, vmem, vmem, vmem],
            out_specs=vmem,
            scratch_shapes=[
                pltpu.VMEM((C * 2, rows, width), jnp.bfloat16),
                pltpu.VMEM((R, depth, cols), jnp.bfloat16),
                pltpu.VMEM((rows, cols), jnp.float32),
                pltpu.VMEM((rows, cols), jnp.float32),
                dma((2,)), dma((C,)), dma((C,)), dma((C,)), dma((C,)),
                dma((R - 1, parts)), dma((R - 1, parts)), dma((R - 1, parts)), dma((R - 1, parts)),
            ],
            compiler_params=pltpu.CompilerParams(
                collective_id=0, has_side_effects=True, vmem_limit_bytes=48 * 2**20),
            cost_estimate=pl.CostEstimate(
                flops=2 * rows * depth * R * cols, bytes_accessed=4 * 2**20, transcendentals=0),
        )(integrals, int_mask, amplitudes, domain_mask,
          virt_energy.reshape(1, rows), occ_energy.reshape(1, cols))

    placed = (
        P("row", ("col", "pair")),
        P("row", ("col", "pair")),
        P("row", ("col", "pair")),
        P("row", ("col", "pair")),
        P("row"),
        P(("col", "pair")),
    )
    return jax.shard_map(
        local, mesh=mesh, in_specs=placed, out_specs=P("row", ("col", "pair")), check_vma=False
    )
```

time: 79.9 us -> 31.7 us (0.40)
  waiting for transfers between devices: 58.2 us -> 0 us
  Pallas kernels: 0 us -> 27.1 us
  between operations: 13.4 us -> 0.01 us
  other arithmetic: 3.9 us -> 0 us
  local copies, waits for them, and re-layouts: 0.68 us -> 4.17 us
  matrix products: 3.37 us -> 0 us
    all_gather x2 -> x0, waiting for transfers between devices: 58.2 us -> none  [the longest x1 29.6 us: local(): lax.all_gather(masked_ints, ('col', 'pair'), axis=1, tiled=True)]
    pallas_call x0 -> x1, Pallas kernels: none -> 27.1 us  [local(): pl.pallas_call(functools.partial(kernel, R, C), out_shape=jax.ShapeDtypeS...]
    unnamed x6 -> x12, local copies, waits for them, and re-layouts: 0.01 us -> 4.17 us
    dot_general x1 -> x0, matrix products: 3.37 us -> none  [local(): jnp.dot(lax.all_gather(masked_ints, ('col', 'pair'), axis=1, tiled=True),...]
    mul x2 -> x0, other arithmetic: 2.44 us -> none  [the longest x1 1.67 us: mask_rows(): shaped * row_mask[:, None, :].astype(values.dtype)]
    convert_element_type x2 -> x0, other arithmetic: 1.46 us -> none  [the longest x1 0.78 us: mask_rows(): row_mask[:, None, :].astype(values.dtype)]
  transfers between devices with their start and end apart: 2 -> 0, of which waited for: 2 -> 0; matrix products, arithmetic and copies ran while one was open for 3% -> 0% of each run, Pallas kernels for 0% -> 0%
where the time goes in v1:
time: 31.7 us; the launch traced here: 31.3 us
  Pallas kernels  27.1 us (85%)
  local copies, waits for them, and re-layouts  4.17 us (13%)
    pallas_call x1, Pallas kernels, local(): pl.pallas_call(functools.partial(kernel, R, C), out_shape=jax.ShapeDtypeS...  27.1 us
    unnamed x12, local copies, waits for them, and re-layouts  4.17 us

profile of v1, /device:TPU:0, one launch (start us, length us, event | category | flops | bytes accessed | tf_op | source)
XLA Modules:
  0.0 31.3 jit_solution(16744221388941606139)
XLA Ops:
  0.0 0.0 copy-start.2
  0.0 0.0 copy-start.4
  0.0 0.8 %copy.7.im_ref = s32[8,4]{1,0:T(8,128)S(1)} copy(s32[8,4]{0,1:T(4,128)} %param.7) | data formatting | bytes 256 | tf_op args[1]
  0.8 0.0 copy-done.2
  0.8 0.0 copy-done.4
  0.8 0.0 copy-start
  0.8 0.9 %copy-done = bf16[512,256]{1,0:T(8,128)(2,1)S(1)} copy-done((bf16[512,256]{1,0:T(8,128)(2,1)S(1)}, bf16[512,256]{1,0:T(8,128)(2,1)}, u32[]{:S(2)}) %copy-start) | copy-done | bytes 262168
  1.7 0.0 copy-start.1
  1.7 0.9 %copy-done.1 = bf16[512,256]{1,0:T(8,128)(2,1)S(1)} copy-done((bf16[512,256]{1,0:T(8,128)(2,1)S(1)}, bf16[512,256]{1,0:T(8,128)(2,1)}, u32[]{:S(2)}) %copy-start.1) | copy-done | bytes 262168
  2.7 0.0 copy-start.3
  2.7 0.7 %copy-done.3 = f32[512]{0:T(512)S(1)} copy-done((f32[512]{0:T(512)S(1)}, f32[512]{0:T(512)}, u32[]{:S(2)}) %copy-start.3) | copy-done | bytes 2072
  3.4 27.1 %shard_map.64 = f32[512,256]{1,0:T(8,128)S(1)} custom-call(bf16[512,256]{1,0:T(8,128)(2,1)S(1)} %copy-done, s32[8,4]{1,0:T(8,128)S(1)} %copy.7.im_ref, bf16[512,256]{1,0:T(8,128)(2,1)S(1)} %copy-done.1, s32[8,256]{1,0:T(8,128)S(1)} %copy-done.2, f32[1,512]{1,0:T(1,128)S(1)} %bitcast.2, f32[1,256]{1,0:T(1,128)S(1)} %bitcast.3), custom_call_target="tpu_custom_call" | custom-call | flops 536870912 | bytes 4194304 | tf_op jit(solution)/shard_map/pallas_call | solution.py:206
  30.5 0.8 %copy.9 = f32[512,256]{1,0:T(8,128)} copy(f32[512,256]{1,0:T(8,128)S(1)} %shard_map.64) | data formatting | bytes 1048576
Async XLA Ops:
  0.0 0.8 %copy-start.2 = (s32[8,256]{1,0:T(8,128)S(1)}, s32[8,256]{1,0:T(8,128)}, u32[]{:S(2)}) copy-start(s32[8,256]{1,0:T(8,128)} %dm_ref.1) | copy-start | bytes 24580
  0.0 0.8 %copy-start.4 = (f32[256]{0:T(256)S(1)}, f32[256]{0:T(256)}, u32[]{:S(2)}) copy-start(f32[256]{0:T(256)} %param.11) | copy-start | bytes 3076
  0.8 1.0 %copy-start = (bf16[512,256]{1,0:T(8,128)(2,1)S(1)}, bf16[512,256]{1,0:T(8,128)(2,1)}, u32[]{:S(2)}) copy-start(bf16[512,256]{1,0:T(8,128)(2,1)} %a_hbm.1) | copy-start | bytes 786436
  1.7 0.9 %copy-start.1 = (bf16[512,256]{1,0:T(8,128)(2,1)S(1)}, bf16[512,256]{1,0:T(8,128)(2,1)}, u32[]{:S(2)}) copy-start(bf16[512,256]{1,0:T(8,128)(2,1)} %b_hbm.1) | copy-start | bytes 786436
  2.7 0.7 %copy-start.3 = (f32[512]{0:T(512)S(1)}, f32[512]{0:T(512)}, u32[]{:S(2)}) copy-start(f32[512]{0:T(512)} %param.10) | copy-start | bytes 6148

commit v2 on v1

v2 whole, which is shorter than its diff:
```python
import functools

import jax
import jax.numpy as jnp
from jax import lax
from jax.experimental import pallas as pl
from jax.experimental.pallas import tpu as pltpu
from jax.sharding import PartitionSpec as P

TILE = 64
MESH = pl.DeviceIdType.MESH


def flipped(index, distance, count):
    out, bit = 0, 1
    while bit < count:
        have = lax.rem(index // bit, 2)
        out = out + bit * (1 - have if (distance // bit) % 2 else have)
        bit *= 2
    return out


def kernel(R, C, a_hbm, im_hbm, b_hbm, dm_hbm, v_hbm, o_hbm, out_ref,
           a_all, b_all, acc, inv, im_ref, dm_ref, v_ref, o_ref, load_sem,
           a_send, a_recv, sib_send, sib_recv, dn_send, dn_recv, up_send, up_recv):
    r, c, p = lax.axis_index("row"), lax.axis_index("col"), lax.axis_index("pair")
    q = 1 - p
    me = c * 2 + p
    rows, width = a_hbm.shape
    depth, cols = b_hbm.shape
    parts = depth // width
    half = rows // 2
    bits = [1 << i for i in range(C.bit_length() - 1)]

    loads = [
        pltpu.make_async_copy(src, dst, load_sem.at[i]) for i, (src, dst) in enumerate([
            (dm_hbm, dm_ref), (b_hbm, b_all.at[r]), (im_hbm, im_ref), (a_hbm, a_all.at[me]),
            (v_hbm, v_ref), (o_hbm, o_ref)])
    ]
    for load in loads:
        load.start()

    others = [flipped(c, d, C) for d in range(C)]
    barrier = pltpu.get_barrier_semaphore()

    def greet(device):
        pl.semaphore_signal(barrier, inc=1, device_id=device, device_id_type=MESH)

    greet((r, c, q))
    for e in bits:
        greet((r, others[e], p))

    @pl.when(r > 0)
    def _():
        greet((r - 1, c, p))

    @pl.when(r < R - 1)
    def _():
        greet((r + 1, c, p))

    def part(block, j):
        return b_all.at[block, pl.ds(j * width, width)]

    def down(block, s, j):
        return pltpu.make_async_remote_copy(
            src_ref=part(block, j), dst_ref=part(block, j),
            send_sem=dn_send.at[s, j], recv_sem=dn_recv.at[s, j],
            device_id=(r - 1, c, p), device_id_type=MESH)

    def up(block, s, j):
        return pltpu.make_async_remote_copy(
            src_ref=part(block, j), dst_ref=part(block, j),
            send_sem=up_send.at[s, j], recv_sem=up_recv.at[s, j],
            device_id=(r + 1, c, p), device_id_type=MESH)

    def across(d, e, h):
        piece = a_all.at[others[d] * 2 + p, pl.ds(h * half, half)]
        return pltpu.make_async_remote_copy(
            src_ref=piece, dst_ref=piece,
            send_sem=a_send.at[d + e, h], recv_sem=a_recv.at[d + e, h],
            device_id=(r, others[e], p), device_id_type=MESH)

    def sibling(d, h, core=None):
        piece = a_all.at[others[d] * 2 + (p if core is None else core), pl.ds(h * half, half)]
        return pltpu.make_async_remote_copy(
            src_ref=piece, dst_ref=piece,
            send_sem=sib_send.at[d, h], recv_sem=sib_recv.at[d, h],
            device_id=(r, c, q), device_id_type=MESH)

    def onward(d, h):
        if d == 0:
            return bits
        low, high = d & -d, 1 << (d.bit_length() - 1)
        return [e for e in bits if (e < low if h == 0 else e > high)]

    def arrives(d, h):
        low, high = d & -d, 1 << (d.bit_length() - 1)
        e = low if h == 0 else high
        piece = a_all.at[others[d] * 2 + p, pl.ds(h * half, half)]
        pltpu.make_async_remote_copy(
            src_ref=piece, dst_ref=piece,
            send_sem=a_send.at[d, h], recv_sem=a_recv.at[d, h],
            device_id=(r, others[e], p), device_id_type=MESH).wait_recv()
        for e in onward(d, h):
            across(d, e, h).start()
        sibling(d, h).start()

    loads[0].wait()
    loads[1].wait()
    for t in range(depth // TILE):
        keep = dm_ref[t:t + 1, :].astype(jnp.bfloat16)
        here = pl.ds(t * TILE, TILE)
        b_all[r, here, :] = b_all[r, here, :] * keep

    pl.semaphore_wait(barrier, 1 + len(bits) + (r + R - 1) // R + (2 * R - 2 - r) // R)

    for j in range(parts):
        @pl.when(r > 0)
        def _():
            down(r, 0, j).start()

        @pl.when(r < R - 1)
        def _():
            up(r, 0, j).start()

    loads[2].wait()
    loads[3].wait()
    lane = lax.broadcasted_iota(jnp.int32, (1, width), 1) // TILE
    for t in range(rows // TILE):
        keep = jnp.zeros((1, width), jnp.float32)
        for u in range(width // TILE):
            keep = jnp.where(lane == u, im_ref[u:u + 1, t:t + 1].astype(jnp.float32), keep)
        here = pl.ds(t * TILE, TILE)
        a_all[me, here, :] = a_all[me, here, :] * keep.astype(jnp.bfloat16)

    for h in (1, 0):
        for e in bits:
            g = h if 2 * e < C else 1 - h
            across(0, e, g).start()
    for h in range(2):
        sibling(0, h).start()

    loads[4].wait()
    loads[5].wait()
    for t in range(rows // 128):
        v = jnp.broadcast_to(v_ref[:, t * 128:(t + 1) * 128], (128, 128)).T
        for u in range(cols // 128):
            lanes = slice(u * 128, (u + 1) * 128)
            factor = 1.0 / (v - o_ref[:, lanes])
            for w in range(128 // TILE):
                row = t * (128 // TILE) + w
                keep = dm_ref[row:row + 1, lanes].astype(jnp.float32)
                inv[pl.ds(row * TILE, TILE), lanes] = factor[w * TILE:(w + 1) * TILE] * keep

    def receive(s, j):
        above, below = r + s + 1, r - s - 1

        @pl.when(above < R)
        def _():
            down(above, s, j).wait_recv()

            @pl.when(r > 0)
            def _():
                down(above, s + 1, j).start()

        @pl.when(below >= 0)
        def _():
            up(below, s, j).wait_recv()

            @pl.when(r < R - 1)
            def _():
                up(below, s + 1, j).start()

    def product(block, j):
        return jnp.dot(a_all[block * parts + j], b_all[block, j * width:(j + 1) * width],
                       preferred_element_type=jnp.float32)

    def add(s, j):
        @pl.when(r + s + 1 < R)
        def _():
            acc[...] += product(r + s + 1, j)

        @pl.when(r - s - 1 >= 0)
        def _():
            acc[...] += product(r - s - 1, j)

    along = [(0, j) for j in range(parts)]
    near = [d for d in range(1, C) if d in bits]
    for h in (1, 0):
        for d in near:
            arrives(d, h if 2 * d < C else 1 - h)
        if along:
            receive(*along.pop(0))
    while along:
        receive(*along.pop(0))
    for d in sorted(range(1, C), key=lambda d: d.bit_count()):
        if d not in near:
            for h in range(2):
                arrives(d, h)
    later = [(s, j) for s in range(1, R - 1) for j in range(parts)]
    if later:
        receive(*later[0])
    for d in range(C):
        for h in range(2):
            sibling(d, h, q).wait_recv()

    acc[...] = product(r, 0)
    for j in range(1, parts):
        acc[...] += product(r, j)
    due = [(0, j) for j in range(parts)]
    for item in later[:1]:
        add(*due.pop(0))
        due.append(item)
    for item in later[1:]:
        if item == later[-1]:
            while due:
                add(*due.pop(0))
        receive(*item)
        due.append(item)
        if item != later[-1]:
            add(*due.pop(0))
    while due:
        add(*due.pop(0))

    out_ref[...] = acc[...] * inv[...]

    for d in range(C):
        for h in range(2):
            sibling(d, h).wait_send()
            for e in onward(d, h):
                across(d, e, h).wait_send()
    for s in range(R - 1):
        for j in range(parts):
            @pl.when((r + s < R) & (r > 0))
            def _():
                down(r + s, s, j).wait_send()

            @pl.when((r - s >= 0) & (r < R - 1))
            def _():
                up(r - s, s, j).wait_send()


def solution(mesh):
    R, C = mesh.shape["row"], mesh.shape["col"]

    def local(integrals, int_mask, amplitudes, domain_mask, virt_energy, occ_energy):
        rows, width = integrals.shape
        depth, cols = amplitudes.shape
        parts = depth // width
        vmem = pl.BlockSpec(memory_space=pltpu.VMEM)
        hbm = pl.BlockSpec(memory_space=pltpu.HBM)
        dma = pltpu.SemaphoreType.DMA
        return pl.pallas_call(
            functools.partial(kernel, R, C),
            out_shape=jax.ShapeDtypeStruct((rows, cols), jnp.float32),
            in_specs=[hbm] * 6,
            out_specs=vmem,
            scratch_shapes=[
                pltpu.VMEM((C * 2, rows, width), jnp.bfloat16),
                pltpu.VMEM((R, depth, cols), jnp.bfloat16),
                pltpu.VMEM((rows, cols), jnp.float32),
                pltpu.VMEM((rows, cols), jnp.float32),
                pltpu.VMEM(int_mask.shape[::-1], jnp.int32),
                pltpu.VMEM(domain_mask.shape, jnp.int32),
                pltpu.VMEM((1, rows), jnp.float32),
                pltpu.VMEM((1, cols), jnp.float32),
                dma((6,)), dma((C, 2)), dma((C, 2)), dma((C, 2)), dma((C, 2)),
                dma((R - 1, parts)), dma((R - 1, parts)), dma((R - 1, parts)), dma((R - 1, parts)),
            ],
            compiler_params=pltpu.CompilerParams(
                collective_id=0, has_side_effects=True, vmem_limit_bytes=48 * 2**20),
            cost_estimate=pl.CostEstimate(
                flops=2 * rows * depth * R * cols, bytes_accessed=4 * 2**20, transcendentals=0),
        )(integrals, int_mask.T, amplitudes, domain_mask,
          virt_energy.reshape(1, rows), occ_energy.reshape(1, cols))

    placed = (
        P("row", ("col", "pair")),
        P("row", ("col", "pair")),
        P("row", ("col", "pair")),
        P("row", ("col", "pair")),
        P("row"),
        P(("col", "pair")),
    )
    return jax.shard_map(
        local, mesh=mesh, in_specs=placed, out_specs=P("row", ("col", "pair")), check_vma=False
    )
```

time: 31.7 us -> 27.5 us (0.87)
  Pallas kernels: 27.1 us -> 23.1 us
    pallas_call x1, Pallas kernels: 27.1 us -> 23.1 us  [local(): pl.pallas_call(functools.partial(kernel, R, C), out_shape=jax.ShapeDtypeS...]
    unnamed x12 -> x13, local copies, waits for them, and re-layouts: 4.17 us -> 4.1 us
where the time goes in v2:
time: 27.5 us; the launch traced here: 27.2 us
  Pallas kernels  23.1 us (84%)
  local copies, waits for them, and re-layouts  4.1 us (15%)
    pallas_call x1, Pallas kernels, local(): pl.pallas_call(functools.partial(kernel, R, C), out_shape=jax.ShapeDtypeS...  23.1 us
    unnamed x13, local copies, waits for them, and re-layouts  4.1 us

profile of v2, /device:TPU:0, one launch (start us, length us, event | category | flops | bytes accessed | tf_op | source)
XLA Modules:
  0.0 27.2 jit_solution(13552051018358231805)
XLA Ops:
  0.0 0.0 copy-start.4
  0.0 0.0 copy-start.3
  0.0 0.0 copy-start.5
  0.0 0.7 %copy-done.4 = f32[512]{0:T(512)S(1)} copy-done((f32[512]{0:T(512)S(1)}, f32[512]{0:T(512)}, u32[]{:S(2)}) %copy-start.4) | copy-done | bytes 2072
  0.7 0.0 copy-done.3
  0.7 0.0 copy-done.5
  0.7 0.0 copy-start
  0.7 0.9 %copy-done = bf16[512,256]{1,0:T(8,128)(2,1)S(1)} copy-done((bf16[512,256]{1,0:T(8,128)(2,1)S(1)}, bf16[512,256]{1,0:T(8,128)(2,1)}, u32[]{:S(2)}) %copy-start) | copy-done | bytes 262168
  1.7 0.0 copy-start.1
  1.7 0.9 %copy-done.1 = bf16[512,256]{1,0:T(8,128)(2,1)S(1)} copy-done((bf16[512,256]{1,0:T(8,128)(2,1)S(1)}, bf16[512,256]{1,0:T(8,128)(2,1)}, u32[]{:S(2)}) %copy-start.1) | copy-done | bytes 262168
  2.6 0.0 copy-start.2
  2.6 0.7 %copy-done.2 = s32[8,256]{1,0:T(8,128)S(1)} copy-done((s32[8,256]{1,0:T(8,128)S(1)}, s32[8,256]{1,0:T(8,128)}, u32[]{:S(2)}) %copy-start.2) | copy-done | bytes 8216
  3.3 23.1 %shard_map.64 = f32[512,256]{1,0:T(8,128)S(1)} custom-call(bf16[512,256]{1,0:T(8,128)(2,1)S(1)} %copy-done, s32[4,8]{1,0:T(4,128)S(1)} %bitcast.3, bf16[512,256]{1,0:T(8,128)(2,1)S(1)} %copy-done.1, s32[8,256]{1,0:T(8,128)S(1)} %copy-done.2, f32[1,512]{1,0:T(1,128)S(1)} %bitcast.4, f32[1,256]{1,0:T(1,128)S(1)} %bitcast.5), custom_call_target="tpu_custom_call" | custom-call | flops 536870912 | bytes 4194304 | tf_op jit(solution)/shard_map/pallas_call | solution.py:253
  26.4 0.8 %copy.8 = f32[512,256]{1,0:T(8,128)} copy(f32[512,256]{1,0:T(8,128)S(1)} %shard_map.64) | data formatting | bytes 1048576
Async XLA Ops:
  0.0 0.7 %copy-start.4 = (f32[512]{0:T(512)S(1)}, f32[512]{0:T(512)}, u32[]{:S(2)}) copy-start(f32[512]{0:T(512)} %param.10) | copy-start | bytes 6148
  0.0 0.7 %copy-start.3 = (s32[8,4]{0,1:T(4,128)S(1)}, s32[8,4]{0,1:T(4,128)}, u32[]{:S(2)}) copy-start(s32[8,4]{0,1:T(4,128)} %param.7) | copy-start | bytes 388
  0.0 0.7 %copy-start.5 = (f32[256]{0:T(256)S(1)}, f32[256]{0:T(256)}, u32[]{:S(2)}) copy-start(f32[256]{0:T(256)} %param.11) | copy-start | bytes 3076
  0.7 0.9 %copy-start = (bf16[512,256]{1,0:T(8,128)(2,1)S(1)}, bf16[512,256]{1,0:T(8,128)(2,1)}, u32[]{:S(2)}) copy-start(bf16[512,256]{1,0:T(8,128)(2,1)} %a_hbm.1) | copy-start | bytes 786436
  1.7 0.9 %copy-start.1 = (bf16[512,256]{1,0:T(8,128)(2,1)S(1)}, bf16[512,256]{1,0:T(8,128)(2,1)}, u32[]{:S(2)}) copy-start(bf16[512,256]{1,0:T(8,128)(2,1)} %b_hbm.1) | copy-start | bytes 786436
  2.6 0.7 %copy-start.2 = (s32[8,256]{1,0:T(8,128)S(1)}, s32[8,256]{1,0:T(8,128)}, u32[]{:S(2)}) copy-start(s32[8,256]{1,0:T(8,128)} %dm_hbm.1) | copy-start | bytes 24580

commit v3 on v2

--- a/solution.py
+++ b/solution.py
@@ -8,6 +8,7 @@
 from jax.sharding import PartitionSpec as P
 
 TILE = 64
+PIECES = 4
 MESH = pl.DeviceIdType.MESH
 
 
@@ -21,7 +22,7 @@
 
 
 def kernel(R, C, a_hbm, im_hbm, b_hbm, dm_hbm, v_hbm, o_hbm, out_ref,
-           a_all, b_all, acc, inv, im_ref, dm_ref, v_ref, o_ref, load_sem,
+           a_all, b_all, acc, inv, im_ref, dm_ref, v_ref, o_ref, load_sem, store_sem,
            a_send, a_recv, sib_send, sib_recv, dn_send, dn_recv, up_send, up_recv):
     r, c, p = lax.axis_index("row"), lax.axis_index("col"), lax.axis_index("pair")
     q = 1 - p
@@ -171,18 +172,20 @@
             def _():
                 up(below, s + 1, j).start()
 
-    def product(block, j):
-        return jnp.dot(a_all[block * parts + j], b_all[block, j * width:(j + 1) * width],
+    whole = pl.ds(0, rows)
+
+    def product(block, j, here=whole):
+        return jnp.dot(a_all[block * parts + j, here, :], b_all[block, j * width:(j + 1) * width],
                        preferred_element_type=jnp.float32)
 
-    def add(s, j):
+    def add(s, j, here=whole):
         @pl.when(r + s + 1 < R)
         def _():
-            acc[...] += product(r + s + 1, j)
+            acc[here, :] += product(r + s + 1, j, here)
 
         @pl.when(r - s - 1 >= 0)
         def _():
-            acc[...] += product(r - s - 1, j)
+            acc[here, :] += product(r - s - 1, j, here)
 
     along = [(0, j) for j in range(parts)]
     near = [d for d in range(1, C) if d in bits]
@@ -219,10 +222,15 @@
         due.append(item)
         if item != later[-1]:
             add(*due.pop(0))
-    while due:
-        add(*due.pop(0))
-
-    out_ref[...] = acc[...] * inv[...]
+
+    stores = []
+    for t in range(PIECES):
+        here = pl.ds(t * (rows // PIECES), rows // PIECES)
+        for s, j in due:
+            add(s, j, here)
+        acc[here, :] = acc[here, :] * inv[here, :]
+        stores.append(pltpu.make_async_copy(acc.at[here], out_ref.at[here], store_sem.at[t]))
+        stores[-1].start()
 
     for d in range(C):
         for h in range(2):
@@ -238,6 +246,8 @@
             @pl.when((r - s >= 0) & (r < R - 1))
             def _():
                 up(r - s, s, j).wait_send()
+    for store in stores:
+        store.wait()
 
 
 def solution(mesh):
@@ -247,14 +257,13 @@
         rows, width = integrals.shape
         depth, cols = amplitudes.shape
         parts = depth // width
-        vmem = pl.BlockSpec(memory_space=pltpu.VMEM)
-        hbm = pl.BlockSpec(memory_space=pltpu.HBM)
+        hbm = pl.BlockSpec(memory_space=pl.ANY)
         dma = pltpu.SemaphoreType.DMA
         return pl.pallas_call(
             functools.partial(kernel, R, C),
             out_shape=jax.ShapeDtypeStruct((rows, cols), jnp.float32),
             in_specs=[hbm] * 6,
-            out_specs=vmem,
+            out_specs=hbm,
             scratch_shapes=[
                 pltpu.VMEM((C * 2, rows, width), jnp.bfloat16),
                 pltpu.VMEM((R, depth, cols), jnp.bfloat16),
@@ -264,11 +273,11 @@
                 pltpu.VMEM(domain_mask.shape, jnp.int32),
                 pltpu.VMEM((1, rows), jnp.float32),
                 pltpu.VMEM((1, cols), jnp.float32),
-                dma((6,)), dma((C, 2)), dma((C, 2)), dma((C, 2)), dma((C, 2)),
+                dma((6,)), dma((PIECES,)), dma((C, 2)), dma((C, 2)), dma((C, 2)), dma((C, 2)),
                 dma((R - 1, parts)), dma((R - 1, parts)), dma((R - 1, parts)), dma((R - 1, parts)),
             ],
             compiler_params=pltpu.CompilerParams(
-                collective_id=0, has_side_effects=True, vmem_limit_bytes=48 * 2**20),
+                collective_id=0, has_side_effects=True, vmem_limit_bytes=62 * 2**20),
             cost_estimate=pl.CostEstimate(
                 flops=2 * rows * depth * R * cols, bytes_accessed=4 * 2**20, transcendentals=0),
         )(integrals, int_mask.T, amplitudes, domain_mask,

time: 27.5 us -> 26.2 us (0.953)
  local copies, waits for them, and re-layouts: 4.1 us -> 1.87 us
  Pallas kernels: 23.1 us -> 24.2 us
    unnamed x13 -> x1, local copies, waits for them, and re-layouts: 4.1 us -> 1.87 us
    pallas_call x1, Pallas kernels: 23.1 us -> 24.2 us  [local(): pl.pallas_call(functools.partial(kernel, R, C), out_shape=jax.ShapeDtypeS...]
where the time goes in v3:
time: 26.2 us; the launch traced here: 26 us
  Pallas kernels  24.2 us (92%)
  local copies, waits for them, and re-layouts  1.87 us (7%)
    pallas_call x1, Pallas kernels, local(): pl.pallas_call(functools.partial(kernel, R, C), out_shape=jax.ShapeDtypeS...  24.2 us
    unnamed x1, local copies, waits for them, and re-layouts  1.87 us

profile of v3, /device:TPU:0, one launch (start us, length us, event | category | flops | bytes accessed | tf_op | source)
XLA Modules:
  0.0 26.0 jit_solution(887039602600311798)
XLA Ops:
  0.0 24.2 %shard_map.64 = f32[512,256]{1,0:T(8,128)} custom-call(bf16[512,256]{1,0:T(8,128)(2,1)} %a_hbm.1, s32[4,8]{1,0:T(4,128)} %bitcast.3, bf16[512,256]{1,0:T(8,128)(2,1)} %b_hbm.1, s32[8,256]{1,0:T(8,128)} %dm_hbm.1, f32[1,512]{1,0:T(1,128)} %bitcast.4, f32[1,256]{1,0:T(1,128)} %bitcast.5), custom_call_target="tpu_custom_call" | custom-call | flops 536870912 | bytes 4194304 | tf_op jit(solution)/shard_map/pallas_call | solution.py:262
  24.2 1.9 %copy.8 = f32[512,256]{1,0:T(8,128)} copy(f32[512,256]{1,0:T(8,128)} %shard_map.64) | data formatting | bytes 1048576

commit v4 on v3

--- a/solution.py
+++ b/solution.py
@@ -8,7 +8,7 @@
 from jax.sharding import PartitionSpec as P
 
 TILE = 64
-PIECES = 4
+PIECES = 1
 MESH = pl.DeviceIdType.MESH
 
 

time: 26.2 us -> 25.9 us (0.989)
  Pallas kernels: 24.2 us -> 23.8 us
    pallas_call x1, Pallas kernels: 24.2 us -> 23.8 us  [local(): pl.pallas_call(functools.partial(kernel, R, C), out_shape=jax.ShapeDtypeS...]
where the time goes in v4:
time: 25.9 us; the launch traced here: 25.7 us
  Pallas kernels  23.8 us (92%)
  local copies, waits for them, and re-layouts  1.87 us (7%)
    pallas_call x1, Pallas kernels, local(): pl.pallas_call(functools.partial(kernel, R, C), out_shape=jax.ShapeDtypeS...  23.8 us
    unnamed x1, local copies, waits for them, and re-layouts  1.87 us

profile of v4, /device:TPU:0, one launch (start us, length us, event | category | flops | bytes accessed | tf_op | source)
XLA Modules:
  0.0 25.7 jit_solution(9616926377465914872)
XLA Ops:
  0.0 23.8 %shard_map.64 = f32[512,256]{1,0:T(8,128)} custom-call(bf16[512,256]{1,0:T(8,128)(2,1)} %a_hbm.1, s32[4,8]{1,0:T(4,128)} %bitcast.3, bf16[512,256]{1,0:T(8,128)(2,1)} %b_hbm.1, s32[8,256]{1,0:T(8,128)} %dm_hbm.1, f32[1,512]{1,0:T(1,128)} %bitcast.4, f32[1,256]{1,0:T(1,128)} %bitcast.5), custom_call_target="tpu_custom_call" | custom-call | flops 536870912 | bytes 4194304 | tf_op jit(solution)/shard_map/pallas_call | solution.py:262
  23.8 1.9 %copy.8 = f32[512,256]{1,0:T(8,128)} copy(f32[512,256]{1,0:T(8,128)} %shard_map.64) | data formatting | bytes 1048576
